TPU v7x, 32 devices: a whole 2x2x4 slice. The times are simulated.
32 devices in a mesh: group: 2 (over y), ep: 4 (over x, core), tp: 4 (over z).
Axes of the slice: x: 2, y: 2, z: 4, core: 2. Of those that a mesh axis runs over, the one named last changes fastest.
Arguments:
- tokens: bfloat16 [192, 3072], P(('group', 'ep', 'tp')), parts along dimension 0, may hold values from -6 to 6
- experts: int32 [192, 2], P(('group', 'ep', 'tp')), parts along dimension 0, may hold values from 0 to 3, as said below
- replicas: int32 [192, 2], P(('group', 'ep', 'tp')), parts along dimension 0, may hold values from 0 to 2, as said below
- gates: float32 [192, 2], P(('group', 'ep', 'tp')), parts along dimension 0, may hold values from 0.1 to 1
- w_gate: bfloat16 [16, 3072, 4096], P('ep', None, 'tp'), may hold values from -0.109375 to 0.109375
- w_up: bfloat16 [16, 3072, 4096], P('ep', None, 'tp'), may hold values from -0.109375 to 0.109375
- w_down: bfloat16 [16, 4096, 3072], P('ep', 'tp'), may hold values from -0.0625 to 0.0625
Outputs:
- moe_output: bfloat16 [192, 3072], P(('group', 'ep', 'tp')), parts along dimension 0
There are 2 independent parts, one for each index of `group`. A program takes and returns all parts, laid end to end along the dimension named above; an argument that names none is the same for every part. Nothing has to cross between parts.
Inputs may be any that keep to these rules, and one draw needn't show every extreme that they name: The two experts of a row differ. `replicas`: a replica above 0 stands only beside an expert below 2; the picks of the rows of one device name one instance at most 2 times, exactly 2 times for some instance on every device; the picks of the rows of all devices with one index of tp name one instance at most 8 times, exactly 8 times for some instance.
All inputs are finite; a program needn't handle non-finite values.
Results may differ from a plain program's by a relative error of at most 0.018.
Values may be sent and summed in bfloat16 or wider, within the bound.
A program may use at most 128 MiB of HBM per device.

v0:
```python
import jax
import jax.numpy as jnp
from jax import lax
from jax.sharding import PartitionSpec as P

SPLIT = 2
CAP = 2


def pack_rows(arrived, arrived_flags, recv_most):
    src_count, local_piece, col_count, depth = arrived_flags.shape
    marked = jnp.transpose(arrived_flags.astype(jnp.float32), (2, 1, 0, 3)).reshape(
        col_count, local_piece, src_count * depth
    )
    before = jnp.cumsum(marked, axis=2) - marked
    places = jnp.arange(recv_most, dtype=jnp.float32)
    select = (before[:, :, None, :] == places[None, None, :, None]) & (marked[:, :, None, :] > 0.5)
    select = select.astype(jnp.bfloat16).reshape(
        col_count, local_piece, recv_most, src_count, depth
    )
    packed = jnp.einsum(
        "tqrec,eqtcd->trqd", select, arrived, preferred_element_type=jnp.float32
    ).astype(jnp.bfloat16)
    return (packed.reshape(col_count * recv_most, local_piece, arrived.shape[-1]), select)


def on_device(tokens, experts, replicas, gates, w_gate, w_up, w_down):
    ep_count = lax.axis_size("ep")
    local_piece = w_gate.shape[0]
    piece_count = local_piece * ep_count
    inst_count = piece_count // SPLIT
    expert_count = inst_count // 2
    hot_count = expert_count // 2
    recv_most = CAP * ep_count
    rows_dev, features = tokens.shape
    slot_total = inst_count * CAP
    instance = jnp.where(
        replicas == 0,
        experts,
        expert_count + (replicas - 1) * hot_count + (experts - 1) % hot_count,
    )
    pick_ids = instance.reshape(-1)
    matching = pick_ids[:, None] == pick_ids[None, :]
    positions = jnp.arange(pick_ids.shape[0])
    earlier = positions[:, None] > positions[None, :]
    slot_idx = jnp.sum((matching & earlier).astype(jnp.int32), axis=1)
    target = pick_ids * CAP + slot_idx
    onehot = (jnp.arange(slot_total)[:, None] == target[None, :]).astype(jnp.float32)
    slot_rows = onehot.reshape(slot_total, rows_dev, 2).sum(axis=2)
    inst_rows = jnp.dot(
        slot_rows.astype(jnp.bfloat16), tokens, preferred_element_type=jnp.float32
    ).astype(jnp.bfloat16)
    send_rows = jnp.repeat(inst_rows.reshape(inst_count, CAP, features), SPLIT, axis=0).reshape(
        ep_count, local_piece, CAP, features
    )
    inst_flags = jnp.sum(slot_rows, axis=1).astype(jnp.bfloat16).reshape(inst_count, CAP)
    send_flags = jnp.repeat(inst_flags, SPLIT, axis=0).reshape(ep_count, local_piece, CAP)
    arrived, arrived_flags = (
        lax.all_to_all(send_rows, "ep", split_axis=0, concat_axis=0, tiled=True),
        lax.all_to_all(send_flags, "ep", split_axis=0, concat_axis=0, tiled=True),
    )
    packed, select = pack_rows(arrived[:, :, None], arrived_flags[:, :, None], recv_most)
    own_select = select[0]
    piece = lax.all_gather(packed, "tp", axis=0, tiled=True)
    gate_act = jnp.einsum("rqd,qdf->rqf", piece, w_gate, preferred_element_type=jnp.float32)
    up_act = jnp.einsum("rqd,qdf->rqf", piece, w_up, preferred_element_type=jnp.float32)
    hidden = (jax.nn.silu(gate_act) * up_act).astype(jnp.bfloat16)
    piece = hidden
    summed = lax.psum_scatter(
        jnp.einsum("rqf,qfd->rqd", piece, w_down, preferred_element_type=jnp.float32).astype(
            jnp.bfloat16
        ),
        "tp",
        scatter_dimension=0,
        tiled=True,
    )
    returning = jnp.einsum(
        "qrec,rqd->eqcd", own_select, summed, preferred_element_type=jnp.float32
    ).astype(jnp.bfloat16)
    returned = lax.all_to_all(returning, "ep", split_axis=0, concat_axis=0, tiled=True)
    halves = returned.reshape(inst_count, SPLIT, CAP, features).astype(jnp.float32)
    returned_rows = jnp.sum(halves, axis=1).reshape(slot_total, features)
    weighted = (onehot * gates.reshape(-1)[None, :]).reshape(slot_total, rows_dev, 2).sum(axis=2)
    mixed = jnp.dot(weighted.T, returned_rows, precision=lax.Precision.HIGHEST)
    return mixed.astype(jnp.bfloat16)


def solution(mesh):
    return jax.shard_map(
        on_device,
        mesh=mesh,
        in_specs=(
            P(("group", "ep", "tp"), None),
            P(("group", "ep", "tp"), None),
            P(("group", "ep", "tp"), None),
            P(("group", "ep", "tp"), None),
            P("ep", None, "tp"),
            P("ep", None, "tp"),
            P("ep", "tp", None),
        ),
        out_specs=P(("group", "ep", "tp"), None),
        check_vma=False,
    )
```

profile of v0, /device:TPU:0, one launch (start us, length us, event | category | flops | bytes accessed | tf_op | source)
XLA Modules:
  0.0 120.0 jit_solution(8980640386766301691)
XLA Ops:
  6.5 0.8 copy.65
  7.3 0.8 copy.62
  8.2 0.2 convert_reduce_fusion.1
  8.4 0.8 copy.66
  9.7 0.6 copy.68
  10.3 4.2 %all-to-all-start.1 = ((bf16[4,4,2]{1,2,0:T(2,128)(2,1)}), bf16[4,4,2]{1,2,0:T(2,128)(2,1)S(1)}, u32[]{:S(2)}, u32[]{:S(2)}) async-start(bf16[4,4,2]{1,2,0:T(2,128)(2,1)} %copy.68), calls=%async_computation.1 | async-start | bytes 4096 | tf_op jit(solution)/shard_map/all_to_all | solution.py:60
  14.5 0.2 convolution_convert_fusion.2
  14.7 3.4 %all-to-all-done.1 = bf16[4,4,2]{1,2,0:T(2,128)(2,1)S(1)} async-done(((bf16[4,4,2]{1,2,0:T(2,128)(2,1)}), bf16[4,4,2]{1,2,0:T(2,128)(2,1)S(1)}, u32[]{:S(2)}, u32[]{:S(2)}) %all-to-all-start.1) | async-done | bytes 96 | tf_op jit(solution)/shard_map/all_to_all | solution.py:60
  18.1 0.8 broadcast_in_dim.4
  18.9 3.4 %all-to-all-start = ((bf16[4,4,2,3072]{3,2,1,0:T(2,128)(2,1)}), bf16[4,4,2,3072]{3,2,1,0:T(2,128)(2,1)S(1)}, u32[]{:S(2)}, u32[]{:S(2)}) async-start(bf16[4,4,2,3072]{3,2,1,0:T(2,128)(2,1)} %bitcast), calls=%async_computation | async-start | bytes 393216 | tf_op jit(solution)/shard_map/all_to_all | solution.py:59
  22.7 4.9 %all-to-all-done = bf16[4,4,2,3072]{3,2,1,0:T(2,128)(2,1)S(1)} async-done(((bf16[4,4,2,3072]{3,2,1,0:T(2,128)(2,1)}), bf16[4,4,2,3072]{3,2,1,0:T(2,128)(2,1)S(1)}, u32[]{:S(2)}, u32[]{:S(2)}) %all-to-all-start) | async-done | bytes 196640 | tf_op jit(solution)/shard_map/all_to_all | solution.py:59
  27.6 0.3 fusion.2
  27.9 20.3 %all-gather = bf16[1,32,4,3072]{3,1,2,0:T(8,128)(2,1)S(1)} all-gather(bf16[1,8,4,3072]{3,1,2,0:T(8,128)(2,1)S(1)} %fusion.2), channel_id=2, replica_groups=mesh['group'=2,'ep'=4,'tp'=4] {'tp'}, dimensions={1}, use_global_device_ids=true | all-gather | bytes 983040 | tf_op jit(solution)/shard_map/all_gather | solution.py:64
  48.2 10.4 %convolution_bitcast_fusion.2 = f32[32,4,1024]{2,0,1:T(8,128)S(1)} fusion(bf16[4,3072,1024]{2,1,0:T(8,128)(2,1)} %param.11, bf16[1,32,4,3072]{3,1,2,0:T(8,128)(2,1)S(1)} %all-gather), kind=kOutput, calls=%fused_computation.10 | convolution fusion | flops 805306368 | bytes 26476544 | tf_op jit(solution)/shard_map/rqd,qdf->rqf/dot_general | solution.py:65
  58.6 10.6 %fusion.5 = bf16[32,4,1024]{2,0,1:T(8,128)(2,1)S(1)} fusion(bf16[4,3072,1024]{2,1,0:T(8,128)(2,1)} %param.12, bf16[1,32,4,3072]{3,1,2,0:T(8,128)(2,1)S(1)} %all-gather, f32[32,4,1024]{2,0,1:T(8,128)S(1)} %convolution_bitcast_fusion.2), kind=kOutput, calls=%fused_computation.12 | convolution fusion | flops 806092800 | bytes 26738688 | tf_op jit(solution)/shard_map/rqd,qdf->rqf/dot_general | solution.py:66
  69.3 10.5 %fusion = bf16[4,4,8,3072]{3,2,1,0:T(8,128)(2,1)S(1)} fusion(bf16[32,4,1024]{2,0,1:T(8,128)(2,1)S(1)} %fusion.5, bf16[4,1024,3072]{2,1,0:T(8,128)(2,1)} %param.13), kind=kOutput, calls=%fused_computation.1 | convolution fusion | flops 805699584 | bytes 26214400 | tf_op jit(solution)/shard_map/rqf,qfd->rqd/dot_general | solution.py:70
  79.8 0.9 copy.80
  80.8 21.9 %reduce-scatter.4.cloned.1.call-done = bf16[8,12288]{1,0:T(8,128)(2,1)} async-done(((bf16[32,12288]{1,0:T(8,128)(2,1)}), bf16[8,12288]{1,0:T(8,128)(2,1)}) %reduce-scatter.4.cloned.1.call-update) | async-done | bytes 196624
  102.7 1.2 fusion.3
  103.9 0.2 copy.76
  104.0 7.9 %all_to_all.15 = bf16[4,4,2,3072]{3,2,1,0:T(2,128)(2,1)S(1)} all-to-all(bf16[4,4,2,3072]{3,2,1,0:T(2,128)(2,1)S(1)} %copy.76), channel_id=1, replica_groups=mesh['group'=2,'ep'=4,'tp'=4] {'ep'}, dimensions={0} | all-to-all | bytes 393216 | tf_op jit(solution)/shard_map/all_to_all | solution.py:80
  111.9 0.2 convert_reduce_fusion
  112.1 0.1 reshape.97
  112.3 0.8 convolution_convert_fusion.3
  (24 shorter events, 1.1 us)
Async XLA Ops:
  6.5 7.9 %copy-start = (bf16[6,3072]{1,0:T(8,128)(2,1)S(1)}, bf16[6,3072]{1,0:T(8,128)(2,1)}, u32[]{:S(2)}) copy-start(bf16[6,3072]{1,0:T(8,128)(2,1)} %param.7) | copy-start | bytes 110596
  10.3 7.9 %all-to-all-start.1 = ((bf16[4,4,2]{1,2,0:T(2,128)(2,1)}), bf16[4,4,2]{1,2,0:T(2,128)(2,1)S(1)}, u32[]{:S(2)}, u32[]{:S(2)}) async-start(bf16[4,4,2]{1,2,0:T(2,128)(2,1)} %copy.68), calls=%async_computation.1 | async-start | bytes 4096 | tf_op jit(solution)/shard_map/all_to_all | solution.py:60
  18.9 8.7 %all-to-all-start = ((bf16[4,4,2,3072]{3,2,1,0:T(2,128)(2,1)}), bf16[4,4,2,3072]{3,2,1,0:T(2,128)(2,1)S(1)}, u32[]{:S(2)}, u32[]{:S(2)}) async-start(bf16[4,4,2,3072]{3,2,1,0:T(2,128)(2,1)} %bitcast), calls=%async_computation | async-start | bytes 393216 | tf_op jit(solution)/shard_map/all_to_all | solution.py:59
  22.3 80.4 %reduce-scatter.4.cloned.1.call-start = ((), (), s32[]{:S(2)}) async-start(), calls=%async_computation.4 | async-start | bytes 983040
Sparse Core Ops, SparseCore 0:
  80.9 21.7 reduce-scatter.3
where the time goes:
time: 120 us
  matrix products  34.1 us (28%)
  waiting for transfers between devices  30.2 us (25%)
  blocking collectives  28.2 us (24%)
  between operations  13.5 us (11%)
  starting transfers between devices  7.61 us (6%)
  local copies, waits for them, and re-layouts  5.67 us (5%)
    unnamed x2, waiting for transfers between devices  22 us
    all_gather x1, blocking collectives, on_device(): piece = lax.all_gather(packed, 'tp', axis=0, tiled=True)  20.3 us
    dot_general x1, matrix products, on_device(): jnp.einsum('rqd,qdf->rqf', piece, w_up, preferred_element_type=jnp.float32)  10.6 us
    dot_general x1, matrix products, on_device(): jnp.einsum('rqf,qfd->rqd', piece, w_down, preferred_element_type=jnp.floa...  10.5 us
    dot_general x1, matrix products, on_device(): jnp.einsum('rqd,qdf->rqf', piece, w_gate, preferred_element_type=jnp.floa...  10.4 us
    all_to_all x1, blocking collectives, on_device(): lax.all_to_all(returning, 'ep', split_axis=0, concat_axis=0, tiled=True)  7.86 us
    all_to_all x1, waiting for transfers between devices, on_device(): lax.all_to_all(send_rows, 'ep', split_axis=0, concat_axis=0, tiled=True)  4.89 us
    all_to_all x1, starting transfers between devices, on_device(): lax.all_to_all(send_flags, 'ep', split_axis=0, concat_axis=0, tiled=True)  4.21 us
  transfers between devices with their start and end apart: 3, of which 3 were waited for; matrix products, arithmetic and copies ran while one was open for 0% of the time, Pallas kernels for 0%

commit v1 on v0

--- a/solution.py
+++ b/solution.py
@@ -1,6 +1,10 @@
+import functools
+
 import jax
 import jax.numpy as jnp
 from jax import lax
+from jax.experimental import pallas as pl
+from jax.experimental.pallas import tpu as pltpu
 from jax.sharding import PartitionSpec as P
 
 SPLIT = 2
@@ -85,9 +89,366 @@
     return mixed.astype(jnp.bfloat16)
 
 
+COLS = 512
+SUB = 8
+F32 = jnp.float32
+BF16 = jnp.bfloat16
+
+
+def iota(shape, dim):
+    return lax.broadcasted_iota(jnp.int32, shape, dim)
+
+
+def fused_kernel(n_tp, slots, tokens_ref, experts_ref, replicas_ref, gates_ref, wg, wu, wd, out_ref,
+                 ring, stage, blocks, x_all, x_sel, hidden, send_a, keep_a, recv_a, send_b, keep_b,
+                 recv_b, send_c, recv_c, w_sem, z_sem, x_sem, c_sem, a_sem, b_sem, t_sem):
+    rows_dev, features = tokens_ref.shape
+    local_piece, _, units = wg.shape
+    local_inst = local_piece // SPLIT
+    n_ep = 4
+    inst_count = local_inst * n_ep
+    expert_count = inst_count // 2
+    hot_count = expert_count // 2
+    per_inst = CAP * n_ep * n_tp
+    segs = features // COLS
+    halves = units // COLS
+    block_rows = stage.shape[0]
+    n_dev = n_ep * n_tp
+    tok_rows = n_dev * SUB
+    steps = local_piece * halves
+    gu_chunks = 2 * steps
+    per_slot = features // units
+
+    e = lax.axis_index("ep")
+    t = lax.axis_index("tp")
+    x, core = e // 2, e % 2
+    x_peer = (1 - x) * 2 + core
+    core_peer = x * 2 + 1 - core
+
+    def gu_copy(step, which):
+        src = wg if which == 0 else wu
+        piece, part = step // halves, step % halves
+        slot = 2 * step + which
+        return pltpu.make_async_copy(
+            src.at[piece, :, pl.ds(pl.multiple_of(part * COLS, COLS), COLS)],
+            ring.at[slot], w_sem.at[slot, 0])
+
+    def down_place(unit):
+        chunk, v = unit // per_slot, unit % per_slot
+        return (gu_chunks + chunk) % slots, v
+
+    def down_copy(unit):
+        slot, v = down_place(unit)
+        col, piece = unit // local_piece, unit % local_piece
+        return pltpu.make_async_copy(
+            wd.at[piece, :, pl.ds(pl.multiple_of(col * COLS, COLS), COLS)],
+            ring.at[slot, pl.ds(pl.multiple_of(v * units, units), units), :],
+            w_sem.at[slot, v])
+
+    down_units = segs * local_piece
+    down_chunks = down_units // per_slot
+    early = min(slots - gu_chunks, down_chunks)
+
+    barrier = pltpu.get_barrier_semaphore()
+    for r in range(1, n_tp):
+        pl.semaphore_signal(barrier, inc=1, device_id={"tp": (t + r) % n_tp},
+                            device_id_type=pl.DeviceIdType.MESH)
+    for peer in (x_peer, core_peer):
+        pl.semaphore_signal(barrier, inc=1, device_id={"ep": peer},
+                            device_id_type=pl.DeviceIdType.MESH)
+
+    def start_weights(step, _):
+        gu_copy(step, 0).start()
+        gu_copy(step, 1).start()
+        return 0
+
+    lax.fori_loop(0, FIRST, start_weights, 0)
+
+    lane = iota((rows_dev, 128), 1)
+    coef = jnp.zeros((rows_dev, 128), F32)
+    for k in range(2):
+        ex = experts_ref[:, k:k + 1]
+        rep = replicas_ref[:, k:k + 1]
+        hot = (ex + (hot_count - 1)) & (hot_count - 1)
+        inst = jnp.where(rep == 0, ex, expert_count + (rep - 1) * hot_count + hot)
+        coef = coef + jnp.where(lane == inst, gates_ref[:, k:k + 1], 0.0)
+    stage[...] = jnp.zeros_like(stage)
+    for s in range(segs):
+        stage[s * rows_dev:(s + 1) * rows_dev, :] = tokens_ref[:, s * COLS:(s + 1) * COLS].astype(F32)
+    rest = coef
+    for j in range(3):
+        part = rest.astype(BF16).astype(F32)
+        stage[segs * rows_dev:(segs + 1) * rows_dev, j * 128:(j + 1) * 128] = part
+        rest = rest - part
+
+    def place(xx, cc, tt):
+        return (cc * 2 + xx) * n_tp + tt
+
+    blocks[place(x, core, t)] = stage[...].astype(BF16)
+    pl.semaphore_wait(barrier, n_tp + 1)
+
+    def to(where, block, sems, i):
+        return pltpu.make_async_remote_copy(
+            src_ref=blocks.at[block], dst_ref=blocks.at[block],
+            send_sem=sems.at[0, i], recv_sem=sems.at[1, i],
+            device_id=where, device_id_type=pl.DeviceIdType.MESH)
+
+    own = [place(x, core, (t + n_tp - r) % n_tp) for r in range(n_tp)]
+    other = [place(1 - x, core, (t + n_tp - r) % n_tp) for r in range(n_tp)]
+    z_copies = [to({"tp": (t + r) % n_tp}, own[0], z_sem, r - 1) for r in range(1, n_tp)]
+    x_copies = [to({"ep": x_peer}, own[r], x_sem, r) for r in range(n_tp)]
+    c_copies = [to({"ep": core_peer}, (own + other)[r], c_sem, r) for r in range(2 * n_tp)]
+    for copy in z_copies:
+        copy.start()
+    x_copies[0].start()
+    c_copies[0].start()
+    lax.fori_loop(FIRST, steps, start_weights, 0)
+    for chunk in range(early):
+        for v in range(per_slot):
+            down_copy(chunk * per_slot + v).start()
+    for r in range(1, n_tp):
+        z_copies[r - 1].wait_recv()
+        x_copies[r].start()
+        c_copies[r].start()
+    for r in range(n_tp):
+        x_copies[r].wait_recv()
+        c_copies[n_tp + r].start()
+    for r in range(2 * n_tp):
+        c_copies[r].wait_recv()
+    for copy in z_copies + x_copies + c_copies:
+        copy.wait_send()
+
+    arrived = blocks[...].reshape(n_dev * block_rows, COLS)
+    pos = iota((tok_rows, n_dev * block_rows), 0)
+    n = pos & (SUB - 1)
+    rel = iota((tok_rows, n_dev * block_rows), 1) - ((pos >> 3) * block_rows + n)
+    rel = jnp.where(n < rows_dev, rel, -1)
+    for s in range(segs + 1):
+        pick = jnp.where(rel == s * rows_dev, 1.0, 0.0).astype(BF16)
+        got = jnp.dot(pick, arrived, preferred_element_type=F32)
+        if s < segs:
+            x_all[:, s * COLS:(s + 1) * COLS] = got.astype(BF16)
+        else:
+            coef_all = got[:, 0:128] + got[:, 128:256] + got[:, 256:384]
+    coef_t = coef_all.T
+    tri = jnp.where(iota((tok_rows, tok_rows), 0) < iota((tok_rows, tok_rows), 1), 1.0, 0.0).astype(BF16)
+    sels, gate_cols = [], []
+    for i in range(local_inst):
+        mine = iota((128, tok_rows), 0) == e * local_inst + i
+        row = jnp.sum(jnp.where(mine, coef_t, 0.0), axis=0, keepdims=True)
+        weight = jnp.broadcast_to(row, (per_inst, tok_rows))
+        marked = jnp.where(weight > 0.0, 1.0, 0.0)
+        before = jnp.dot(marked.astype(BF16), tri, preferred_element_type=F32)
+        sel = jnp.where(before == iota((per_inst, tok_rows), 0).astype(F32), marked, 0.0)
+        gate_cols.append(jnp.sum(sel * weight, axis=1, keepdims=True))
+        sels.append(sel)
+    sel_all = jnp.concatenate(sels, axis=0)
+    spread = sel_all.T.astype(BF16)
+    sel_bf = sel_all.astype(BF16)
+    for s in range(segs):
+        x_sel[:, :, s * COLS:(s + 1) * COLS] = jnp.dot(
+            sel_bf, x_all[:, s * COLS:(s + 1) * COLS], preferred_element_type=F32
+        ).astype(BF16).reshape(local_inst, per_inst, COLS)
+
+    def up_step(step, _):
+        piece, part = step // halves, step % halves
+        rows = x_sel[piece // SPLIT]
+        gu_copy(step, 0).wait()
+        g = jnp.dot(rows, ring[2 * step], preferred_element_type=F32)
+        gu_copy(step, 1).wait()
+        u = jnp.dot(rows, ring[2 * step + 1], preferred_element_type=F32)
+        h = g / (1.0 + jnp.exp(-g)) * u
+        hidden[piece, :, pl.ds(pl.multiple_of(part * COLS, COLS), COLS)] = h.astype(BF16)
+        for j in range(2):
+            chunk = early + 2 * step + j
+
+            @pl.when(chunk < down_chunks)
+            def _():
+                for v in range(per_slot):
+                    down_copy(chunk * per_slot + v).start()
+        return 0
+
+    lax.fori_loop(0, steps, up_step, 0)
+
+    half = tok_rows // 2
+    quarter = tok_rows // 4
+
+    def a_copy(c):
+        return pltpu.make_async_remote_copy(
+            src_ref=send_a.at[c], dst_ref=recv_a.at[c],
+            send_sem=a_sem.at[0, c], recv_sem=a_sem.at[1, c],
+            device_id={"ep": core_peer}, device_id_type=pl.DeviceIdType.MESH)
+
+    def b_copy(c):
+        return pltpu.make_async_remote_copy(
+            src_ref=send_b.at[c], dst_ref=recv_b.at[c],
+            send_sem=b_sem.at[0, c], recv_sem=b_sem.at[1, c],
+            device_id={"ep": x_peer}, device_id_type=pl.DeviceIdType.MESH)
+
+    def t_copy(c, r):
+        peer = (t + r) % n_tp
+        return pltpu.make_async_remote_copy(
+            src_ref=send_c.at[c, peer], dst_ref=recv_c.at[c, r - 1],
+            send_sem=t_sem.at[0, c, r - 1], recv_sem=t_sem.at[1, c, r - 1],
+            device_id={"tp": peer}, device_id_type=pl.DeviceIdType.MESH)
+
+    def stage_a(c):
+        parts = []
+        for i in range(local_inst):
+            total = jnp.zeros((per_inst, COLS), F32)
+            for h in range(SPLIT):
+                piece = i * SPLIT + h
+                unit = c * local_piece + piece
+                slot, v = down_place(unit)
+                down_copy(unit).wait()
+                total = total + jnp.dot(
+                    hidden[piece], ring[slot, pl.ds(pl.multiple_of(v * units, units), units), :],
+                    preferred_element_type=F32)
+            parts.append((total * gate_cols[i]).astype(BF16))
+        y = jnp.dot(spread, jnp.concatenate(parts, axis=0), preferred_element_type=F32)
+        low, high = y[:half], y[half:]
+        send_a[c] = jnp.where(core == 0, high, low).astype(BF16)
+        keep_a[c] = jnp.where(core == 0, low, high)
+        a_copy(c).start()
+
+    def stage_b(c):
+        a_copy(c).wait_recv()
+        v = keep_a[c] + recv_a[c].astype(F32)
+        low, high = v[:quarter], v[quarter:]
+        send_b[c] = jnp.where(x == 0, high, low).astype(BF16)
+        keep_b[c] = jnp.where(x == 0, low, high)
+        b_copy(c).start()
+
+    def stage_c(c):
+        b_copy(c).wait_recv()
+        v = keep_b[c] + recv_b[c].astype(F32)
+        keep_b[c] = v
+        for tt in range(n_tp):
+            rows = v[tt * SUB:(tt + 1) * SUB]
+            send_c[c, tt] = jnp.concatenate(
+                [rows[:, :COLS // 2], rows[:, COLS // 2:]], axis=0).astype(BF16)
+        for r in range(1, n_tp):
+            t_copy(c, r).start()
+
+    def finish(c):
+        rows = keep_b[c, pl.ds(pl.multiple_of(t * SUB, SUB), SUB), :]
+        for r in range(1, n_tp):
+            t_copy(c, r).wait_recv()
+            got = recv_c[c, r - 1].astype(F32)
+            rows = rows + jnp.concatenate([got[:SUB], got[SUB:]], axis=1)
+        out_ref[:, pl.ds(pl.multiple_of(c * COLS, COLS), COLS)] = rows[:rows_dev].astype(BF16)
+
+    def down_step(c, _):
+        stage_a(c)
+        for lag, fn in ((1, stage_b), (2, stage_c), (3, finish)):
+            @pl.when(c >= lag)
+            def _():
+                fn(c - lag)
+        return 0
+
+    lax.fori_loop(0, segs, down_step, 0)
+    stage_b(segs - 1)
+    stage_c(segs - 2)
+    stage_c(segs - 1)
+    for c in range(segs - 3, segs):
+        finish(c)
+
+    def drain(c, _):
+        a_copy(c).wait_send()
+        b_copy(c).wait_send()
+        for r in range(1, n_tp):
+            t_copy(c, r).wait_send()
+        return 0
+
+    lax.fori_loop(0, segs, drain, 0)
+
+
+FIRST = 2
+
+
+def fused(n_tp, slots, tokens, experts, replicas, gates, w_gate, w_up, w_down):
+    rows_dev, features = tokens.shape
+    local_piece, _, units = w_gate.shape
+    n_ep = 4
+    local_inst = local_piece // SPLIT
+    per_inst = CAP * n_ep * n_tp
+    n_dev = n_ep * n_tp
+    segs = features // COLS
+    block_rows = -(-(segs + 1) * rows_dev // 16) * 16
+    tok_rows = n_dev * SUB
+    per_slot = features // units
+    vm = pl.BlockSpec(memory_space=pltpu.VMEM)
+    hbm = pl.BlockSpec(memory_space=pl.ANY)
+    dma = pltpu.SemaphoreType.DMA
+    weights = 3 * local_piece * features * units
+    return pl.pallas_call(
+        functools.partial(fused_kernel, n_tp, slots),
+        out_shape=jax.ShapeDtypeStruct((rows_dev, features), BF16),
+        in_specs=[vm] * 4 + [hbm] * 3,
+        out_specs=vm,
+        scratch_shapes=[
+            pltpu.VMEM((slots, features, COLS), BF16),
+            pltpu.VMEM((block_rows, COLS), F32),
+            pltpu.VMEM((n_dev, block_rows, COLS), BF16),
+            pltpu.VMEM((tok_rows, features), BF16),
+            pltpu.VMEM((local_inst, per_inst, features), BF16),
+            pltpu.VMEM((local_piece, per_inst, units), BF16),
+            pltpu.VMEM((segs, tok_rows // 2, COLS), BF16),
+            pltpu.VMEM((segs, tok_rows // 2, COLS), F32),
+            pltpu.VMEM((segs, tok_rows // 2, COLS), BF16),
+            pltpu.VMEM((segs, tok_rows // 4, COLS), BF16),
+            pltpu.VMEM((segs, tok_rows // 4, COLS), F32),
+            pltpu.VMEM((segs, tok_rows // 4, COLS), BF16),
+            pltpu.VMEM((segs, n_tp, 2 * SUB, COLS // 2), BF16),
+            pltpu.VMEM((segs, n_tp - 1, 2 * SUB, COLS // 2), BF16),
+            dma((slots, per_slot)),
+            dma((2, n_tp - 1)),
+            dma((2, n_tp)),
+            dma((2, 2 * n_tp)),
+            dma((2, segs)),
+            dma((2, segs)),
+            dma((2, segs, n_tp - 1)),
+        ],
+        compiler_params=pltpu.CompilerParams(
+            collective_id=0, has_side_effects=True, vmem_limit_bytes=VMEM_LIMIT
+        ),
+        cost_estimate=pl.CostEstimate(
+            flops=2 * weights * per_inst, bytes_accessed=2 * weights, transcendentals=0
+        ),
+    )(tokens, experts, replicas, gates, w_gate, w_up, w_down)
+
+
+VMEM_LIMIT = 64 * 1024 * 1024 - 256 * 1024
+
+
+def slots_for(n_ep, n_tp, tokens, w_gate):
+    rows_dev, features = tokens.shape
+    local_piece, _, units = w_gate.shape
+    if n_ep != 4 or n_tp < 2 or local_piece % SPLIT or rows_dev > SUB:
+        return 0
+    hot = local_piece * n_ep // SPLIT // 4
+    if features % COLS or units % COLS or features % units or hot & (hot - 1) or n_ep * n_tp * SUB != 128:
+        return 0
+    chunks = 2 * local_piece * (units // COLS)
+    down = (features // COLS) * local_piece
+    if down % (features // units):
+        return 0
+    slots = (56 << 20) // (2 * features * COLS)
+    slots = min(slots, chunks + down // (features // units))
+    if slots < chunks or chunks + down // (features // units) > slots + chunks:
+        return 0
+    return slots
+
+
+def layer(n_ep, n_tp, tokens, experts, replicas, gates, w_gate, w_up, w_down):
+    slots = slots_for(n_ep, n_tp, tokens, w_gate)
+    args = (tokens, experts, replicas, gates, w_gate, w_up, w_down)
+    return fused(n_tp, slots, *args) if slots else on_device(*args)
+
+
 def solution(mesh):
     return jax.shard_map(
-        on_device,
+        functools.partial(layer, mesh.shape["ep"], mesh.shape["tp"]),
         mesh=mesh,
         in_specs=(
             P(("group", "ep", "tp"), None),

time: 120 us -> 56.6 us (0.47)
  Pallas kernels: 0 us -> 50.8 us
  matrix products: 34.1 us -> 0 us
  waiting for transfers between devices: 30.2 us -> 0 us
  blocking collectives: 28.2 us -> 0 us
  between operations: 13.5 us -> 0.01 us
  starting transfers between devices: 7.61 us -> 0 us
    pallas_call x0 -> x1, Pallas kernels: none -> 50.8 us  [fused(): pl.pallas_call(functools.partial(fused_kernel, n_tp, slots), out_shape=ja...]
    dot_general x7 -> x0, matrix products: 34.1 us -> none  [the longest x1 10.6 us: on_device(): jnp.einsum('rqd,qdf->rqf', piece, w_up, preferred_element_type=jnp.float32)]
    unnamed x2 -> x0, waiting for transfers between devices: 22 us -> none
    all_gather x1 -> x0, blocking collectives: 20.3 us -> none  [on_device(): piece = lax.all_gather(packed, 'tp', axis=0, tiled=True)]
    all_to_all x2 -> x0, waiting for transfers between devices: 8.29 us -> none  [the longest x1 4.89 us: on_device(): lax.all_to_all(send_rows, 'ep', split_axis=0, concat_axis=0, tiled=True)]
    all_to_all x1 -> x0, blocking collectives: 7.86 us -> none  [on_device(): lax.all_to_all(returning, 'ep', split_axis=0, concat_axis=0, tiled=True)]
    all_to_all x2 -> x0, starting transfers between devices: 7.57 us -> none  [the longest x1 4.21 us: on_device(): lax.all_to_all(send_flags, 'ep', split_axis=0, concat_axis=0, tiled=True)]
    unnamed x6 -> x4, local copies, waits for them, and re-layouts: 3.24 us -> 5.47 us
  transfers between devices with their start and end apart: 3 -> 0, of which waited for: 3 -> 0; matrix products, arithmetic and copies ran while one was open for 0% -> 0% of each run, Pallas kernels for 0% -> 0%
where the time goes in v1:
time: 56.6 us; the launch traced here: 56.3 us
  Pallas kernels  50.8 us (90%)
  local copies, waits for them, and re-layouts  5.47 us (10%)
    pallas_call x1, Pallas kernels, fused(): pl.pallas_call(functools.partial(fused_kernel, n_tp, slots), out_shape=ja...  50.8 us
    unnamed x4, local copies, waits for them, and re-layouts  5.47 us

profile of v1, /device:TPU:0, one launch (start us, length us, event | category | flops | bytes accessed | tf_op | source)
XLA Modules:
  0.0 56.3 jit_solution(5574190420798566528)
XLA Ops:
  0.0 1.4 %copy.8.experts_ref = s32[6,2]{1,0:T(8,128)} copy(s32[6,2]{0,1:T(2,128)} %param.8) | data formatting | bytes 96 | tf_op args[1]
  1.4 1.3 %copy.9.replicas_ref = s32[6,2]{1,0:T(8,128)} copy(s32[6,2]{0,1:T(2,128)} %param.9) | data formatting | bytes 96 | tf_op args[2]
  2.7 1.3 %copy.10.gates_ref = f32[6,2]{1,0:T(8,128)} copy(f32[6,2]{0,1:T(2,128)} %param.10) | data formatting | bytes 96 | tf_op args[3]
  4.0 50.8 %shard_map.73 = bf16[6,3072]{1,0:T(8,128)(2,1)} custom-call(bf16[6,3072]{1,0:T(8,128)(2,1)} %tokens_ref.1, s32[6,2]{1,0:T(8,128)} %copy.8.experts_ref, s32[6,2]{1,0:T(8,128)} %copy.9.replicas_ref, f32[6,2]{1,0:T(8,128)} %copy.10.gates_ref, bf16[4,3072,1024]{2,1,0:T(8,128)(2,1)} %wg.1, bf16[4,3072,1024]{2,1,0:T(8,128)(2,1)} %wu.1, bf16[4,1024,3072]{2,1,0:T(8,128)(2,1)} %wd.1), custom_call_target="tpu_custom_call" | custom-call | flops 2415919104 | bytes 75497472 | tf_op jit(solution)/shard_map/pallas_call | solution.py:384
  54.9 1.4 %copy.12 = bf16[6,3072]{1,0:T(8,128)(2,1)} copy(bf16[6,3072]{1,0:T(8,128)(2,1)} %shard_map.73) | data formatting | bytes 73728

commit v2 on v1

--- a/solution.py
+++ b/solution.py
@@ -164,14 +164,15 @@
 
     lax.fori_loop(0, FIRST, start_weights, 0)
 
-    lane = iota((rows_dev, 128), 1)
-    coef = jnp.zeros((rows_dev, 128), F32)
+    line = iota((128, rows_dev), 0)
+    coef = jnp.zeros((128, rows_dev), F32)
     for k in range(2):
-        ex = experts_ref[:, k:k + 1]
-        rep = replicas_ref[:, k:k + 1]
+        ex = experts_ref[k:k + 1, :]
+        rep = replicas_ref[k:k + 1, :]
         hot = (ex + (hot_count - 1)) & (hot_count - 1)
         inst = jnp.where(rep == 0, ex, expert_count + (rep - 1) * hot_count + hot)
-        coef = coef + jnp.where(lane == inst, gates_ref[:, k:k + 1], 0.0)
+        coef = coef + jnp.where(line == inst, gates_ref[k:k + 1, :], 0.0)
+    coef = coef.T
     stage[...] = jnp.zeros_like(stage)
     for s in range(segs):
         stage[s * rows_dev:(s + 1) * rows_dev, :] = tokens_ref[:, s * COLS:(s + 1) * COLS].astype(F32)
@@ -202,17 +203,28 @@
         copy.start()
     x_copies[0].start()
     c_copies[0].start()
-    lax.fori_loop(FIRST, steps, start_weights, 0)
-    for chunk in range(early):
-        for v in range(per_slot):
-            down_copy(chunk * per_slot + v).start()
+    started = FIRST
+
+    def start_more(upto):
+        upto = min(upto, steps)
+        for step in range(started, upto):
+            start_weights(step, 0)
+        return max(started, upto)
+
+    started = start_more(started + 1)
     for r in range(1, n_tp):
         z_copies[r - 1].wait_recv()
         x_copies[r].start()
         c_copies[r].start()
+        started = start_more(started + 1)
     for r in range(n_tp):
         x_copies[r].wait_recv()
         c_copies[n_tp + r].start()
+        started = start_more(started + 1)
+    started = start_more(steps)
+    for chunk in range(early):
+        for v in range(per_slot):
+            down_copy(chunk * per_slot + v).start()
     for r in range(2 * n_tp):
         c_copies[r].wait_recv()
     for copy in z_copies + x_copies + c_copies:
@@ -363,7 +375,7 @@
     lax.fori_loop(0, segs, drain, 0)
 
 
-FIRST = 2
+FIRST = 1
 
 
 def fused(n_tp, slots, tokens, experts, replicas, gates, w_gate, w_up, w_down):
@@ -415,7 +427,7 @@
         cost_estimate=pl.CostEstimate(
             flops=2 * weights * per_inst, bytes_accessed=2 * weights, transcendentals=0
         ),
-    )(tokens, experts, replicas, gates, w_gate, w_up, w_down)
+    )(tokens, experts.T, replicas.T, gates.T, w_gate, w_up, w_down)
 
 
 VMEM_LIMIT = 64 * 1024 * 1024 - 256 * 1024

time: 56.6 us -> 52.5 us (0.928)
  local copies, waits for them, and re-layouts: 5.47 us -> 1.42 us
    unnamed x4 -> x1, local copies, waits for them, and re-layouts: 5.47 us -> 1.42 us
where the time goes in v2:
time: 52.5 us; the launch traced here: 52.3 us
  Pallas kernels  50.9 us (97%)
  local copies, waits for them, and re-layouts  1.42 us (3%)
    pallas_call x1, Pallas kernels, fused(): pl.pallas_call(functools.partial(fused_kernel, n_tp, slots), out_shape=ja...  50.9 us
    unnamed x1, local copies, waits for them, and re-layouts  1.42 us

profile of v2, /device:TPU:0, one launch (start us, length us, event | category | flops | bytes accessed | tf_op | source)
XLA Modules:
  0.0 52.3 jit_solution(17984764101875505542)
XLA Ops:
  0.0 50.9 %shard_map.73 = bf16[6,3072]{1,0:T(8,128)(2,1)} custom-call(bf16[6,3072]{1,0:T(8,128)(2,1)} %tokens_ref.1, s32[2,6]{1,0:T(2,128)} %bitcast.3, s32[2,6]{1,0:T(2,128)} %bitcast.4, f32[2,6]{1,0:T(2,128)} %bitcast.5, bf16[4,3072,1024]{2,1,0:T(8,128)(2,1)} %wg.1, bf16[4,3072,1024]{2,1,0:T(8,128)(2,1)} %wu.1, bf16[4,1024,3072]{2,1,0:T(8,128)(2,1)} %wd.1), custom_call_target="tpu_custom_call" | custom-call | flops 2415919104 | bytes 75497472 | tf_op jit(solution)/shard_map/pallas_call | solution.py:396
  50.9 1.4 %copy.9 = bf16[6,3072]{1,0:T(8,128)(2,1)} copy(bf16[6,3072]{1,0:T(8,128)(2,1)} %shard_map.73) | data formatting | bytes 73728

commit v3 on v2

--- a/solution.py
+++ b/solution.py
@@ -352,17 +352,19 @@
 
     def down_step(c, _):
         stage_a(c)
-        for lag, fn in ((1, stage_b), (2, stage_c), (3, finish)):
+        for lag, fn in ((LAG_B, stage_b), (LAG_C, stage_c)):
             @pl.when(c >= lag)
             def _():
                 fn(c - lag)
         return 0
 
     lax.fori_loop(0, segs, down_step, 0)
-    stage_b(segs - 1)
-    stage_c(segs - 2)
-    stage_c(segs - 1)
-    for c in range(segs - 3, segs):
+    for c in range(segs, segs + LAG_C):
+        if 0 <= c - LAG_B < segs:
+            stage_b(c - LAG_B)
+        if 0 <= c - LAG_C < segs:
+            stage_c(c - LAG_C)
+    for c in range(segs):
         finish(c)
 
     def drain(c, _):
@@ -376,6 +378,8 @@
 
 
 FIRST = 1
+LAG_B = 3
+LAG_C = 5
 
 
 def fused(n_tp, slots, tokens, experts, replicas, gates, w_gate, w_up, w_down):

time: 52.5 us -> 49.4 us (0.941)
  Pallas kernels: 50.9 us -> 47.7 us
    pallas_call x1, Pallas kernels: 50.9 us -> 47.7 us  [fused(): pl.pallas_call(functools.partial(fused_kernel, n_tp, slots), out_shape=ja...]
where the time goes in v3:
time: 49.4 us; the launch traced here: 49.1 us
  Pallas kernels  47.7 us (97%)
  local copies, waits for them, and re-layouts  1.42 us (3%)
    pallas_call x1, Pallas kernels, fused(): pl.pallas_call(functools.partial(fused_kernel, n_tp, slots), out_shape=ja...  47.7 us
    unnamed x1, local copies, waits for them, and re-layouts  1.42 us

profile of v3, /device:TPU:0, one launch (start us, length us, event | category | flops | bytes accessed | tf_op | source)
XLA Modules:
  0.0 49.1 jit_solution(2552328512242463741)
XLA Ops:
  0.0 47.7 %shard_map.73 = bf16[6,3072]{1,0:T(8,128)(2,1)} custom-call(bf16[6,3072]{1,0:T(8,128)(2,1)} %tokens_ref.1, s32[2,6]{1,0:T(2,128)} %bitcast.3, s32[2,6]{1,0:T(2,128)} %bitcast.4, f32[2,6]{1,0:T(2,128)} %bitcast.5, bf16[4,3072,1024]{2,1,0:T(8,128)(2,1)} %wg.1, bf16[4,3072,1024]{2,1,0:T(8,128)(2,1)} %wu.1, bf16[4,1024,3072]{2,1,0:T(8,128)(2,1)} %wd.1), custom_call_target="tpu_custom_call" | custom-call | flops 2415919104 | bytes 75497472 | tf_op jit(solution)/shard_map/pallas_call | solution.py:400
  47.7 1.4 %copy.9 = bf16[6,3072]{1,0:T(8,128)(2,1)} copy(bf16[6,3072]{1,0:T(8,128)(2,1)} %shard_map.73) | data formatting | bytes 73728

commit v4 on v3

--- a/solution.py
+++ b/solution.py
@@ -100,7 +100,7 @@
 
 
 def fused_kernel(n_tp, slots, tokens_ref, experts_ref, replicas_ref, gates_ref, wg, wu, wd, out_ref,
-                 ring, stage, blocks, x_all, x_sel, hidden, send_a, keep_a, recv_a, send_b, keep_b,
+                 ring, stage, blocks, picks, x_all, x_sel, hidden, send_a, keep_a, recv_a, send_b, keep_b,
                  recv_b, send_c, recv_c, w_sem, z_sem, x_sem, c_sem, a_sem, b_sem, t_sem):
     rows_dev, features = tokens_ref.shape
     local_piece, _, units = wg.shape
@@ -212,6 +212,12 @@
         return max(started, upto)
 
     started = start_more(started + 1)
+    pos = iota((tok_rows, n_dev * block_rows), 0)
+    n = pos & (SUB - 1)
+    rel = iota((tok_rows, n_dev * block_rows), 1) - ((pos >> 3) * block_rows + n)
+    rel = jnp.where(n < rows_dev, rel, -1)
+    for s in range(segs + 1):
+        picks[s] = jnp.where(rel == s * rows_dev, 1.0, 0.0).astype(BF16)
     for r in range(1, n_tp):
         z_copies[r - 1].wait_recv()
         x_copies[r].start()
@@ -231,13 +237,8 @@
         copy.wait_send()
 
     arrived = blocks[...].reshape(n_dev * block_rows, COLS)
-    pos = iota((tok_rows, n_dev * block_rows), 0)
-    n = pos & (SUB - 1)
-    rel = iota((tok_rows, n_dev * block_rows), 1) - ((pos >> 3) * block_rows + n)
-    rel = jnp.where(n < rows_dev, rel, -1)
     for s in range(segs + 1):
-        pick = jnp.where(rel == s * rows_dev, 1.0, 0.0).astype(BF16)
-        got = jnp.dot(pick, arrived, preferred_element_type=F32)
+        got = jnp.dot(picks[s], arrived, preferred_element_type=F32)
         if s < segs:
             x_all[:, s * COLS:(s + 1) * COLS] = got.astype(BF16)
         else:
@@ -406,6 +407,7 @@
             pltpu.VMEM((slots, features, COLS), BF16),
             pltpu.VMEM((block_rows, COLS), F32),
             pltpu.VMEM((n_dev, block_rows, COLS), BF16),
+            pltpu.VMEM((segs + 1, tok_rows, n_dev * block_rows), BF16),
             pltpu.VMEM((tok_rows, features), BF16),
             pltpu.VMEM((local_inst, per_inst, features), BF16),
             pltpu.VMEM((local_piece, per_inst, units), BF16),

time: 49.4 us -> 49.4 us (level)
  no operation moved by 1% of the time
where the time goes in v4:
time: 49.4 us; the launch traced here: 49.1 us
  Pallas kernels  47.7 us (97%)
  local copies, waits for them, and re-layouts  1.42 us (3%)
    pallas_call x1, Pallas kernels, fused(): pl.pallas_call(functools.partial(fused_kernel, n_tp, slots), out_shape=ja...  47.7 us
    unnamed x1, local copies, waits for them, and re-layouts  1.42 us

profile of v4, /device:TPU:0, one launch (start us, length us, event | category | flops | bytes accessed | tf_op | source)
XLA Modules:
  0.0 49.1 jit_solution(13173561806136467610)
XLA Ops:
  0.0 47.7 %shard_map.73 = bf16[6,3072]{1,0:T(8,128)(2,1)} custom-call(bf16[6,3072]{1,0:T(8,128)(2,1)} %tokens_ref.1, s32[2,6]{1,0:T(2,128)} %bitcast.3, s32[2,6]{1,0:T(2,128)} %bitcast.4, f32[2,6]{1,0:T(2,128)} %bitcast.5, bf16[4,3072,1024]{2,1,0:T(8,128)(2,1)} %wg.1, bf16[4,3072,1024]{2,1,0:T(8,128)(2,1)} %wu.1, bf16[4,1024,3072]{2,1,0:T(8,128)(2,1)} %wd.1), custom_call_target="tpu_custom_call" | custom-call | flops 2415919104 | bytes 75497472 | tf_op jit(solution)/shard_map/pallas_call | solution.py:401
  47.7 1.4 %copy.9 = bf16[6,3072]{1,0:T(8,128)(2,1)} copy(bf16[6,3072]{1,0:T(8,128)(2,1)} %shard_map.73) | data formatting | bytes 73728
